TPU v7x, 256 devices: a whole 4x4x8 slice. The times are simulated.
256 devices in a mesh: cuts: 4 (over z_hi, core), member: 16 (over y, z_lo), grid: 4 (over x).
Axes of the slice: x: 4, y: 4, z: 8 (z_hi: 2, z_lo: 4; z = z_hi * 4 + z_lo), core: 2. Of those that a mesh axis runs over, the one named last changes fastest.
Arguments:
- hidden: bfloat16 [4, 16, 8192, 1024], P('cuts', 'member', 'grid'), may hold values from -6 to 6
- noise_seeds: int32 [16], P('member'), may hold values from 0 to 63
- noise_table: float32 [64, 1024], replicated, may hold values from -4 to 4
- inner_weight: bfloat16 [1024, 1024], replicated, may hold values from -0.1875 to 0.1875
- inner_bias: float32 [1024], replicated, may hold values from -3 to 3
- output_weight: bfloat16 [100, 1024], replicated, may hold values from -0.1875 to 0.1875
- output_bias: float32 [100], replicated, may hold values from -3 to 3
- state_bank: float32 [8, 100, 4, 16, 128], P(None, None, 'grid', 'member'), may hold values from -6 to 6
- ic_index: int32 [4], P('cuts'), may hold values from 0 to 7
- target_index: int32 [4], P('cuts'), may hold values from 0 to 7
- area_weight: float32 [4, 16, 128], P('grid', 'member'), may hold values from 0.1 to 1
Outputs:
- inner_weight_grad: float32 [1024, 1024], replicated
- inner_bias_grad: float32 [1024], replicated
- output_weight_grad: float32 [100, 1024], replicated
- output_bias_grad: float32 [100], replicated
- loss: float32 [], replicated
All inputs are finite; a program needn't handle non-finite values.
Results may differ from a plain program's by a relative error of at most 0.0037.
Values may be sent and summed in bfloat16 or wider, within the bound.
A program may use at most 128 MiB of HBM per device.

v0:
```python
import jax
import jax.numpy as jnp
from jax import lax
from jax.sharding import PartitionSpec as P

FAIR_ALPHA = 0.95


def body(
    hidden,
    noise_seeds,
    noise_table,
    inner_weight,
    inner_bias,
    output_weight,
    output_bias,
    state_bank,
    ic_index,
    target_index,
    area_weight,
):
    members_here = hidden.shape[1]
    points_here = hidden.shape[2]
    hidden_width = hidden.shape[3]
    variables = output_weight.shape[0]
    seed_ids = jnp.arange(noise_table.shape[0], dtype=jnp.int32)
    seeds_onehot = (noise_seeds[:, None] == seed_ids[None, :]).astype(jnp.float32)
    noise_rows = jnp.dot(
        seeds_onehot,
        noise_table,
        precision=lax.Precision.HIGHEST,
        preferred_element_type=jnp.float32,
    )
    noisy = (hidden[0].astype(jnp.float32) + noise_rows[:, None, :]).astype(jnp.bfloat16)
    noisy = noisy.reshape(members_here * points_here, hidden_width)
    pre_act = jnp.dot(noisy, inner_weight, preferred_element_type=jnp.float32) + inner_bias
    activation, gelu_back = jax.vjp(jax.nn.gelu, pre_act)
    activation = activation.astype(jnp.bfloat16)
    prediction = (
        lax.dot_general(
            output_weight, activation, (((1,), (1,)), ((), ())), preferred_element_type=jnp.float32
        )
        + output_bias[:, None]
    )
    prediction = prediction.reshape(variables, members_here, points_here)
    point_pred = lax.all_to_all(prediction, "member", split_axis=2, concat_axis=1, tiled=True)
    member_count = point_pred.shape[1]
    flat_bank = state_bank[:, :, 0, 0, :]
    ic_state = lax.dynamic_index_in_dim(flat_bank, ic_index[0], 0, keepdims=False)
    truth_field = lax.dynamic_index_in_dim(flat_bank, target_index[0], 0, keepdims=False)
    ensemble = point_pred + ic_state[:, None, :]
    point_weight = area_weight[0, 0]
    sample_count = lax.axis_size("cuts") * hidden.shape[0]
    total_points = lax.axis_size("grid") * points_here
    epsilon = (1.0 - FAIR_ALPHA) / member_count
    pair_scale = (1.0 - epsilon) / (member_count * (member_count - 1.0))
    errors = ensemble - truth_field[:, None, :]
    differences = ensemble[:, :, None, :] - ensemble[:, None, :, :]
    skill_sum = jnp.sum(jnp.abs(errors), axis=1)
    spread_sum = jnp.sum(jnp.abs(differences), axis=(1, 2))
    sign_sums = jnp.sum(jnp.sign(differences), axis=2)
    crps_field = skill_sum / member_count - 0.5 * pair_scale * spread_sum
    local_loss = jnp.sum(point_weight * crps_field) / (sample_count * total_points * variables)
    member_grad = (
        point_weight / sample_count * (jnp.sign(errors) / member_count - pair_scale * sign_sums)
    ).astype(jnp.bfloat16)
    returned = lax.all_to_all(member_grad, "member", split_axis=1, concat_axis=2, tiled=True)
    returned = returned.reshape(variables, members_here * points_here)
    grad_b2 = jnp.sum(returned.astype(jnp.float32), axis=1)
    grad_w2 = jnp.dot(returned, activation, preferred_element_type=jnp.float32)
    carried = lax.dot_general(
        returned, output_weight, (((0,), (0,)), ((), ())), preferred_element_type=jnp.float32
    )
    pre_grad = gelu_back(carried)[0].astype(jnp.bfloat16)
    grad_b1 = jnp.sum(pre_grad.astype(jnp.float32), axis=0)
    grad_w1 = lax.dot_general(
        noisy, pre_grad, (((0,), (0,)), ((), ())), preferred_element_type=jnp.float32
    )
    grad_w1, grad_b1, grad_w2, grad_b2, loss = lax.psum(
        (grad_w1, grad_b1, grad_w2, grad_b2, local_loss), ("cuts", "member", "grid")
    )
    return (grad_w1, grad_b1, grad_w2, grad_b2, loss)


def solution(mesh):
    return jax.shard_map(
        body,
        mesh=mesh,
        in_specs=(
            P("cuts", "member", "grid", None),
            P("member"),
            P(),
            P(),
            P(),
            P(),
            P(),
            P(None, None, "grid", "member", None),
            P("cuts"),
            P("cuts"),
            P("grid", "member", None),
        ),
        out_specs=(P(), P(), P(), P(), P()),
        check_vma=False,
    )
```

profile of v0, /device:TPU:97, one launch (start us, length us, event | category | flops | bytes accessed | tf_op | source)
XLA Modules:
  0.0 390.6 jit_solution(8578856110412567470)
XLA Ops:
  7.2 0.0 copy-start
  8.0 1.2 fusion.15
  9.1 0.0 copy-done
  9.1 0.0 copy-start.4
  9.1 0.0 copy-start.5
  9.2 11.4 %multiply_convert_fusion = (bf16[2048,1024]{1,0:T(8,128)(2,1)S(1)}, f32[2048,1024]{1,0:T(8,128)}) fusion(f32[1024]{0:T(1024)} %param.15, bf16[1024,1024]{1,0:T(8,128)(2,1)S(1)} %copy-done, bf16[1,1,2048,1024]{3,2,1,0:T(8,128)(2,1)} %param.11, f32[1024]{0:T(1024)S(1)} %bitcast.54), kind=kOutput, calls=%fused_computation.16 | convolution fusion | flops 4322230272 | bytes 18882560 | tf_op jit(solution)/shard_map/dot_general | solution.py:36
  20.6 0.0 copy-start.1
  20.6 0.0 copy-start.6
  20.6 2.0 copy-done.1
  22.6 0.0 copy-done.4
  22.6 0.0 copy-done.5
  22.6 1.4 fusion.14
  24.1 1.9 copy.23
  26.0 7.2 %all-to-all-start = ((f32[100,1,2048]{0,1,2:T(1,128)}), f32[100,1,2048]{0,1,2:T(1,128)S(1)}, u32[]{:S(2)}, u32[]{:S(2)}) async-start(f32[100,1,2048]{0,1,2:T(1,128)} %copy.23), calls=%async_computation | async-start | bytes 2097152 | tf_op jit(solution)/shard_map/all_to_all | solution.py:46
  33.2 0.2 all-reduce.4.cloned.1.call-start
  34.7 0.9 constant_dynamic-slice_fusion.1
  35.6 0.0 copy-done.6
  35.6 21.7 %all-to-all-done = f32[100,1,2048]{0,1,2:T(1,128)S(1)} async-done(((f32[100,1,2048]{0,1,2:T(1,128)}), f32[100,1,2048]{0,1,2:T(1,128)S(1)}, u32[]{:S(2)}, u32[]{:S(2)}) %all-to-all-start) | async-done | bytes 819232 | tf_op jit(solution)/shard_map/all_to_all | solution.py:46
  57.3 0.0 copy-start.8
  57.3 1.4 copy.27
  58.7 0.0 copy-start.2
  58.7 1.6 abs_reduce_fusion
  60.3 7.5 %fusion.1 = (f32[100,128]{1,0:T(8,128)S(1)}, f32[100,16,128]{2,1,0:T(8,128)S(1)}) fusion(f32[100,16,128]{2,1,0:T(8,128)S(1)} %get-tuple-element.13), kind=kLoop, calls=%fused_computation.3 | loop fusion | flops 16166400 | bytes 1689600 | tf_op jit(solution)/shard_map/reduce_sum | solution.py:60
  67.8 0.4 multiply_convert_fusion.1
  68.2 0.1 copy.25
  68.3 17.2 %all_to_all.21 = bf16[100,16,128]{2,0,1:T(8,128)(2,1)S(1)} all-to-all(bf16[100,16,128]{2,0,1:T(8,128)(2,1)S(1)} %copy.25), channel_id=1, replica_groups=mesh['cuts'=4,'member'=16,'grid'=4] {'member'}, dimensions={1} | all-to-all | bytes 819200 | tf_op jit(solution)/shard_map/all_to_all | solution.py:67
  85.5 0.1 copy.26
  85.6 0.1 copy.30
  85.7 0.0 copy-done.2
  85.7 1.5 fusion.20
  87.2 0.0 copy-done.8
  87.2 0.0 copy-start.7
  87.2 9.0 %convert_reduce_fusion = (f32[1024]{0:T(1024)S(1)}, bf16[2048,1024]{1,0:T(8,128)(2,1)S(1)}) fusion(f32[2048,1024]{1,0:T(8,128)} %get-tuple-element.17, f32[1024]{0:T(1024)S(1)} %copy-done.8, bf16[100,2048]{1,0:T(8,128)(2,1)S(1)} %bitcast.49, bf16[100,1024]{1,0:T(8,128)(2,1)S(1)} %copy-done.4), kind=kOutput, calls=%fused_computation.15 | convolution fusion | flops 467663872 | bytes 13205504 | tf_op jit(solution)/shard_map/dot_general | solution.py:71
  96.2 0.0 copy-done.7
  96.2 6.1 %fusion.10 = f32[1024,1024]{1,0:T(8,128)} fusion(bf16[2048,1024]{1,0:T(8,128)(2,1)S(1)} %get-tuple-element.19, bf16[1,1,2048,1024]{3,2,1,0:T(8,128)(2,1)S(1)} %copy-done.7, f32[1024]{0:T(1024)S(1)} %bitcast.55), kind=kOutput, calls=%fused_computation.17 | convolution fusion | flops 4301258752 | bytes 12587008 | tf_op jit(solution)/shard_map/dot_general | solution.py:76
  102.3 0.0 all-reduce.4.cloned.1.call-update
  102.3 0.6 multiply_reduce_fusion
  103.6 0.1 convert_reduce_fusion.1
  103.7 79.0 %all-reduce = (f32[1024]{0:T(1024)}, f32[100]{0:T(128)}, f32[]{:T(128)}) all-reduce(f32[1024]{0:T(1024)S(1)} %get-tuple-element.18, f32[100]{0:T(128)S(1)} %convert_reduce_fusion.1, f32[]{:T(128)S(6)} %div.27), channel_id=1, replica_groups=mesh['cuts'=4,'member'=16,'grid'=4] {'cuts','member','grid'}, use_global_device_ids=true, to_apply=%region_3.4 | all-reduce | flops 1125 | bytes 9000 | tf_op jit(solution)/shard_map/psum | solution.py:79
  182.7 195.4 %all-reduce.4.cloned.1.call-done = (f32[1024,1024]{1,0:T(8,128)}, f32[100,1024]{1,0:T(8,128)}) async-done(((f32[1024,1024]{1,0:T(8,128)}, f32[100,1024]{1,0:T(8,128)}), (f32[1024,1024]{1,0:T(8,128)}, f32[100,1024]{1,0:T(8,128)})) %all-reduce.4.cloned.1.call-update) | async-done | bytes 4603920 | tf_op jit(solution)/shard_map/psum | solution.py:79
  378.2 0.0 copy-start.3
  378.2 4.8 %copy.40 = f32[1024,1024]{1,0:T(8,128)} copy(f32[1024,1024]{1,0:T(8,128)} %get-tuple-element.20) | data formatting | bytes 8388608
  383.0 0.0 copy-done.3
  383.0 0.8 copy.41
  (4 shorter events, 0.0 us)
Async XLA Ops:
  7.2 2.0 copy-start
  9.1 13.5 %copy-start.4 = (bf16[100,1024]{1,0:T(8,128)(2,1)S(1)}, bf16[100,1024]{1,0:T(8,128)(2,1)}, u32[]{:S(2)}) copy-start(bf16[100,1024]{1,0:T(8,128)(2,1)} %param.16) | copy-start | bytes 614404
  9.1 13.5 %copy-start.5 = (f32[100]{0:T(128)S(1)}, f32[100]{0:T(128)}, u32[]{:S(2)}) copy-start(f32[100]{0:T(128)} %param.17) | copy-start | bytes 1204
  20.6 2.0 copy-start.1
  20.6 15.0 %copy-start.6 = (f32[1,1,128]{2,1,0:T(1,128)S(1)}, f32[1,1,128]{2,1,0:T(1,128)}, u32[]{:S(2)}) copy-start(f32[1,1,128]{2,1,0:T(1,128)} %param.21) | copy-start | bytes 1540
  26.0 31.4 %all-to-all-start = ((f32[100,1,2048]{0,1,2:T(1,128)}), f32[100,1,2048]{0,1,2:T(1,128)S(1)}, u32[]{:S(2)}, u32[]{:S(2)}) async-start(f32[100,1,2048]{0,1,2:T(1,128)} %copy.23), calls=%async_computation | async-start | bytes 2097152 | tf_op jit(solution)/shard_map/all_to_all | solution.py:46
  33.2 345.0 %all-reduce.4.cloned.1.call-start = ((), (), s32[]{:S(2)}) async-start(), calls=%async_computation.2 | async-start | bytes 9240576 | tf_op jit(solution)/shard_map/psum | solution.py:79
  57.3 29.9 %copy-start.8 = (f32[1024]{0:T(1024)S(1)}, f32[1024]{0:T(1024)}, u32[]{:S(2)}) copy-start(f32[1024]{0:T(1024)} %param.15) | copy-start | bytes 12292
  58.7 27.0 %copy-start.2 = (bf16[2048,1024]{1,0:T(8,128)(2,1)S(1)}, bf16[2048,1024]{1,0:T(8,128)(2,1)}, u32[]{:S(2)}) copy-start(bf16[2048,1024]{1,0:T(8,128)(2,1)} %copy-done.1) | copy-start | bytes 12582916
  87.2 9.0 %copy-start.7 = (bf16[1,1,2048,1024]{3,2,1,0:T(8,128)(2,1)S(1)}, bf16[1,1,2048,1024]{3,2,1,0:T(8,128)(2,1)}, u32[]{:S(2)}) copy-start(bf16[1,1,2048,1024]{3,2,1,0:T(8,128)(2,1)} %param.11) | copy-start | bytes 12582916
  378.2 4.8 %copy-start.3 = (f32[100,1024]{1,0:T(8,128)S(1)}, f32[100,1024]{1,0:T(8,128)}, u32[]{:S(2)}) copy-start(f32[100,1024]{1,0:T(8,128)} %get-tuple-element.22) | copy-start | bytes 1228804
Sparse Core Ops, SparseCore 0:
  102.4 275.6 all-reduce.3
where the time goes:
time: 391 us
  waiting for transfers between devices  217 us (55%)
  blocking collectives  96.2 us (25%)
  matrix products  30.6 us (8%)
  between operations  16.9 us (4%)
  local copies, waits for them, and re-layouts  12.1 us (3%)
  other arithmetic  10.2 us (3%)
  starting transfers between devices  7.4 us (2%)
    psum x1, waiting for transfers between devices, body(): lax.psum((grad_w1, grad_b1, grad_w2, grad_b2, local_loss), ('cuts', 'memb...  195 us
    psum x1, blocking collectives, body(): lax.psum((grad_w1, grad_b1, grad_w2, grad_b2, local_loss), ('cuts', 'memb...  79 us
    all_to_all x1, waiting for transfers between devices, body(): lax.all_to_all(prediction, 'member', split_axis=2, concat_axis=1, tiled=T...  21.7 us
    all_to_all x1, blocking collectives, body(): lax.all_to_all(member_grad, 'member', split_axis=1, concat_axis=2, tiled=...  17.2 us
    dot_general x1, matrix products, body(): jnp.dot(noisy, inner_weight, preferred_element_type=jnp.float32)  11.4 us
    dot_general x1, matrix products, body(): lax.dot_general(returned, output_weight, (((0,), (0,)), ((), ())), prefer...  8.97 us
  transfers between devices with their start and end apart: 2, of which 2 were waited for; matrix products, arithmetic and copies ran while one was open for 0% of the time, Pallas kernels for 0%

commit v1 on v0

--- a/solution.py
+++ b/solution.py
@@ -77,7 +77,7 @@
         noisy, pre_grad, (((0,), (0,)), ((), ())), preferred_element_type=jnp.float32
     )
     grad_w1, grad_b1, grad_w2, grad_b2, loss = lax.psum(
-        (grad_w1, grad_b1, grad_w2, grad_b2, local_loss), ("cuts", "member", "grid")
+        lax.psum((grad_w1, grad_b1, grad_w2, grad_b2, local_loss), ("member", "grid")), "cuts"
     )
     return (grad_w1, grad_b1, grad_w2, grad_b2, loss)
 

time: 391 us -> 1080 us (2.76)
  waiting for transfers between devices: 217 us -> 682 us
  blocking collectives: 96.2 us -> 313 us
    psum x1 -> x2, waiting for transfers between devices: 195 us -> 660 us  [the longest x1 660 us: body(): lax.psum((grad_w1, grad_b1, grad_w2, grad_b2, local_loss), ('member', 'gr...]
    psum x1 -> x2, blocking collectives: 79 us -> 295 us  [the longest x1 182 us: body(): lax.psum((grad_w1, grad_b1, grad_w2, grad_b2, local_loss), ('member', 'gr...]
  transfers between devices with their start and end apart: 2 -> 3, of which waited for: 2 -> 2; matrix products, arithmetic and copies ran while one was open for 0% -> 0% of each run, Pallas kernels for 0% -> 0%
where the time goes in v1:
time: 1080 us; the launch traced here: 1070 us
  waiting for transfers between devices  682 us (63%)
  blocking collectives  313 us (29%)
  matrix products  30.6 us (3%)
  between operations  16.9 us (2%)
  local copies, waits for them, and re-layouts  12.1 us (1%)
    psum x1, waiting for transfers between devices, body(): lax.psum((grad_w1, grad_b1, grad_w2, grad_b2, local_loss), ('member', 'gr...  660 us
    psum x1, blocking collectives, body(): lax.psum((grad_w1, grad_b1, grad_w2, grad_b2, local_loss), ('member', 'gr...  182 us
    psum x1, blocking collectives, body(): lax.psum(lax.psum((grad_w1, grad_b1, grad_w2, grad_b2, local_loss), ('mem...  113 us
    all_to_all x1, waiting for transfers between devices, body(): lax.all_to_all(prediction, 'member', split_axis=2, concat_axis=1, tiled=T...  21.7 us
  transfers between devices with their start and end apart: 3, of which 2 were waited for; matrix products, arithmetic and copies ran while one was open for 0% of the time, Pallas kernels for 0%

profile of v1, /device:TPU:97, one launch (start us, length us, event | category | flops | bytes accessed | tf_op | source)
XLA Modules:
  0.0 1072.1 jit_solution(4926426083944261445)
XLA Ops:
  7.2 0.0 copy-start
  8.0 1.2 fusion.15
  9.1 0.0 copy-done
  9.1 0.0 copy-start.4
  9.1 0.0 copy-start.5
  9.2 11.4 %multiply_convert_fusion = (bf16[2048,1024]{1,0:T(8,128)(2,1)S(1)}, f32[2048,1024]{1,0:T(8,128)}) fusion(f32[1024]{0:T(1024)} %param.15, bf16[1024,1024]{1,0:T(8,128)(2,1)S(1)} %copy-done, bf16[1,1,2048,1024]{3,2,1,0:T(8,128)(2,1)} %param.11, f32[1024]{0:T(1024)S(1)} %bitcast.54), kind=kOutput, calls=%fused_computation.16 | convolution fusion | flops 4322230272 | bytes 18882560 | tf_op jit(solution)/shard_map/dot_general | solution.py:36
  20.6 0.0 copy-start.1
  20.6 0.0 copy-start.6
  20.6 2.0 copy-done.1
  22.6 0.0 copy-done.4
  22.6 0.0 copy-done.5
  22.6 1.4 fusion.14
  24.1 1.9 copy.23
  26.0 7.2 all-to-all-start
  33.2 0.2 all-reduce.7.cloned.1.call-start
  34.7 0.9 constant_dynamic-slice_fusion.1
  35.6 0.0 copy-done.6
  35.6 21.7 %all-to-all-done = f32[100,1,2048]{0,1,2:T(1,128)S(1)} async-done(((f32[100,1,2048]{0,1,2:T(1,128)}), f32[100,1,2048]{0,1,2:T(1,128)S(1)}, u32[]{:S(2)}, u32[]{:S(2)}) %all-to-all-start) | async-done | bytes 819232 | tf_op jit(solution)/shard_map/all_to_all | solution.py:46
  57.3 0.0 copy-start.8
  57.3 1.4 copy.27
  58.7 0.0 copy-start.2
  58.7 1.6 abs_reduce_fusion
  60.3 7.5 fusion.1
  67.8 0.4 multiply_convert_fusion.1
  68.2 0.1 copy.25
  68.3 17.2 %all_to_all.21 = bf16[100,16,128]{2,0,1:T(8,128)(2,1)S(1)} all-to-all(bf16[100,16,128]{2,0,1:T(8,128)(2,1)S(1)} %copy.25), channel_id=1, replica_groups=mesh['cuts'=4,'member'=16,'grid'=4] {'member'}, dimensions={1} | all-to-all | bytes 819200 | tf_op jit(solution)/shard_map/all_to_all | solution.py:67
  85.5 0.1 copy.26
  85.6 0.1 copy.30
  85.7 0.0 copy-done.2
  85.7 1.5 fusion.20
  87.2 0.0 copy-done.8
  87.2 0.0 copy-start.7
  87.2 9.0 convert_reduce_fusion
  96.2 0.0 copy-done.7
  96.2 6.1 fusion.10
  102.3 0.0 all-reduce.7.cloned.1.call-update
  102.3 0.0 all-reduce.9.cloned.1.call-start
  102.4 660.4 %all-reduce.7.cloned.1.call-done = (f32[1024,1024]{1,0:T(8,128)}, f32[100,1024]{1,0:T(8,128)}) async-done(((f32[1024,1024]{1,0:T(8,128)}, f32[100,1024]{1,0:T(8,128)}), (f32[1024,1024]{1,0:T(8,128)}, f32[100,1024]{1,0:T(8,128)})) %all-reduce.7.cloned.1.call-update) | async-done | bytes 4603920 | tf_op jit(solution)/shard_map/psum | solution.py:80
  762.8 0.0 all-reduce.9.cloned.1.call-update
  762.8 0.6 multiply_reduce_fusion
  764.1 0.1 convert_reduce_fusion.1
  764.2 182.3 %all-reduce = (f32[1024]{0:T(1024)S(1)}, f32[100]{0:T(128)S(1)}, f32[]{:T(128)}) all-reduce(f32[1024]{0:T(1024)S(1)} %get-tuple-element.23, f32[100]{0:T(128)S(1)} %convert_reduce_fusion.1, f32[]{:T(128)S(6)} %div.27), channel_id=1, replica_groups=mesh['cuts'=4,'member'=16,'grid'=4] {'member','grid'}, use_global_device_ids=true, to_apply=%region_4.5 | all-reduce | flops 1125 | bytes 9000 | tf_op jit(solution)/shard_map/psum | solution.py:80
  946.5 113.2 %all-reduce.2 = (f32[1024]{0:T(1024)}, f32[100]{0:T(128)}, f32[]{:T(128)}) all-reduce(f32[1024]{0:T(1024)S(1)} %get-tuple-element.7, f32[100]{0:T(128)S(1)} %get-tuple-element.8, f32[]{:T(128)} %get-tuple-element.9), channel_id=1, replica_groups=mesh['cuts'=4,'member'=16,'grid'=4] {'cuts'}, use_global_device_ids=true, to_apply=%region_5.6 | all-reduce | flops 1125 | bytes 9000 | tf_op jit(solution)/shard_map/psum | solution.py:79
  1059.7 0.0 all-reduce.9.cloned.1.call-done
  1059.7 0.0 copy-start.3
  1059.7 4.8 copy.42
  1064.5 0.0 copy-done.3
  1064.5 0.8 copy.43
  (4 shorter events, 0.0 us)
Async XLA Ops:
  7.2 2.0 copy-start
  9.1 13.5 %copy-start.4 = (bf16[100,1024]{1,0:T(8,128)(2,1)S(1)}, bf16[100,1024]{1,0:T(8,128)(2,1)}, u32[]{:S(2)}) copy-start(bf16[100,1024]{1,0:T(8,128)(2,1)} %param.16) | copy-start | bytes 614404
  9.1 13.5 %copy-start.5 = (f32[100]{0:T(128)S(1)}, f32[100]{0:T(128)}, u32[]{:S(2)}) copy-start(f32[100]{0:T(128)} %param.17) | copy-start | bytes 1204
  20.6 2.0 copy-start.1
  20.6 15.0 %copy-start.6 = (f32[1,1,128]{2,1,0:T(1,128)S(1)}, f32[1,1,128]{2,1,0:T(1,128)}, u32[]{:S(2)}) copy-start(f32[1,1,128]{2,1,0:T(1,128)} %param.21) | copy-start | bytes 1540
  26.0 31.4 %all-to-all-start = ((f32[100,1,2048]{0,1,2:T(1,128)}), f32[100,1,2048]{0,1,2:T(1,128)S(1)}, u32[]{:S(2)}, u32[]{:S(2)}) async-start(f32[100,1,2048]{0,1,2:T(1,128)} %copy.23), calls=%async_computation | async-start | bytes 2097152 | tf_op jit(solution)/shard_map/all_to_all | solution.py:46
  33.2 729.6 %all-reduce.7.cloned.1.call-start = ((), (), s32[]{:S(2)}) async-start(), calls=%async_computation.2 | async-start | bytes 9240576 | tf_op jit(solution)/shard_map/psum | solution.py:80
  57.3 29.9 %copy-start.8 = (f32[1024]{0:T(1024)S(1)}, f32[1024]{0:T(1024)}, u32[]{:S(2)}) copy-start(f32[1024]{0:T(1024)} %param.15) | copy-start | bytes 12292
  58.7 27.0 %copy-start.2 = (bf16[2048,1024]{1,0:T(8,128)(2,1)S(1)}, bf16[2048,1024]{1,0:T(8,128)(2,1)}, u32[]{:S(2)}) copy-start(bf16[2048,1024]{1,0:T(8,128)(2,1)} %copy-done.1) | copy-start | bytes 12582916
  87.2 9.0 copy-start.7
  102.3 957.4 %all-reduce.9.cloned.1.call-start = ((), (), s32[]{:S(2)}) async-start(), calls=%async_computation.3 | async-start | bytes 9240576 | tf_op jit(solution)/shard_map/psum | solution.py:79
  1059.7 4.8 copy-start.3
Sparse Core Ops, SparseCore 0:
  102.4 660.2 all-reduce.6
  765.5 241.1 all-reduce.8
